TPU v7x, 32 devices: a whole 2x2x4 slice. The times are simulated.
32 devices in a mesh: kpt: 2 (over y), state: 8 (over z, x), dom: 2 (over core).
Axes of the slice: x: 2, y: 2, z: 4, core: 2. Of those that a mesh axis runs over, the one named last changes fastest.
Arguments:
- previous: float32 [1024, 16, 4, 128], P(('kpt', 'state'), 'dom'), parts along dimension 0, may hold values from -6 to 6
- current: float32 [1024, 16, 4, 128], P(('kpt', 'state'), 'dom'), parts along dimension 0, may hold values from -6 to 6
- potential: float32 [16, 4, 128], P('dom'), may hold values from -3 to 1
- degree: int32 [1024], P(('kpt', 'state')), parts along dimension 0, may hold values from 1 to 16
- panel_index: int32 [2], P('kpt'), parts along dimension 0, may hold values from 0 to 7
Outputs:
- filtered: float32 [1024, 16, 4, 128], P(('kpt', 'state'), 'dom'), parts along dimension 0
- margin: float32 [128, 512], P(('kpt', 'dom'), 'state'), parts along dimension 0
There are 2 independent parts, one for each index of `kpt`. A program takes and returns all parts, laid end to end along the dimension named above; an argument that names none is the same for every part. Nothing has to cross between parts.
All inputs are finite; a program needn't handle non-finite values.
Results may differ from a plain program's by a relative error of at most 0.00011.
Values sent between devices are 32-bit elements; how exact they have to be, the bound alone decides.
A program may use at most 128 MiB of HBM per device.

v0:
```python
import functools

import jax
import jax.numpy as jnp
import numpy as np
from jax import lax
from jax.experimental import pallas as pl
from jax.experimental.pallas import tpu as pltpu
from jax.sharding import PartitionSpec as P

stencil_weights = (
    -5369.0 / 1800.0,
    12.0 / 7.0,
    -15.0 / 56.0,
    10.0 / 189.0,
    -1.0 / 112.0,
    2.0 / 1925.0,
    -1.0 / 16632.0,
)
spectrum_center = 8.0
spectrum_half = 8.0
first_ratio = 8.0 / (-0.5 - 8.0)
inverse_two = 2.0 / first_ratio
GROUP = 8


def sigma_table(degree):
    sigma_now = jnp.full(degree.shape, first_ratio, jnp.float32)
    for repeat in range(1, 16):
        sigma_now = jnp.where(repeat < degree, 1.0 / (inverse_two - sigma_now), sigma_now)
    sigma_next = 1.0 / (inverse_two - sigma_now)
    sigma_after = 1.0 / (inverse_two - sigma_next)
    return (sigma_now, sigma_next, sigma_after)


def circulant_row(length):
    row = np.zeros(length)
    for m in range(1, len(stencil_weights)):
        row[m % length] += -0.5 * stencil_weights[m]
        row[-m % length] += -0.5 * stencil_weights[m]
    return row


def z_matrix(length):
    row = circulant_row(length)
    full = np.stack([np.roll(row, i) for i in range(length)]).astype(np.float32)
    high = full.astype(jnp.bfloat16)
    low = (full - high.astype(np.float32)).astype(jnp.bfloat16)
    zero = np.zeros_like(high)
    return np.block([[high, low], [high, zero]])


def split(value):
    high = value.astype(jnp.bfloat16)
    low = (value - high.astype(jnp.float32)).astype(jnp.bfloat16)
    return high, low


def kernel(
    sizes,
    root_ref, cur, prev, pot, coef, zmat, out, margin,
    curf, prevf, potf, potb, tcur, tmid, zterm, full, own, slots, panel, parted, partial, other,
    in_local, in_send, in_recv, back_local, back_send, back_recv,
    rs_send, rs_recv, ag_send, ag_recv, piece_sem, out_sem, sum_send, sum_recv,
):
    orbs, nx, ny, nz, states = sizes
    rows = nx // 2 * ny
    half = orbs // 2 * rows
    piece = orbs // states * rows
    dom, state = lax.axis_index("dom"), lax.axis_index("state")
    mate = 1 - dom

    barrier = pltpu.get_barrier_semaphore()
    pl.semaphore_signal(barrier, 1, device_id={"dom": mate}, device_id_type=pl.DeviceIdType.MESH)

    def greet(k, carry):
        pl.semaphore_signal(
            barrier, 1, device_id={"state": lax.rem(state + k, states)}, device_id_type=pl.DeviceIdType.MESH
        )
        return carry

    lax.fori_loop(1, states, greet, 0)
    pl.semaphore_wait(barrier, states)

    coming = []
    spans = ((cur, curf, half), (prev, prevf, half))
    for i, (source, target, size) in enumerate(spans):
        here = target.at[pl.ds(dom * size, size)]
        coming.append(pltpu.make_async_copy(source.at[pl.ds(dom * size, size)], here, in_local.at[i]))
        coming.append(
            pltpu.make_async_remote_copy(
                source.at[pl.ds(mate * size, size)], here, in_send.at[i], in_recv.at[i],
                device_id={"dom": mate}, device_id_type=pl.DeviceIdType.MESH,
            )
        )
    here = potf.at[pl.ds(dom * rows, rows)]
    coming.append(pltpu.make_async_copy(pot, here, in_local.at[2]))
    coming.append(
        pltpu.make_async_remote_copy(
            pot, here, in_send.at[2], in_recv.at[2], device_id={"dom": mate}, device_id_type=pl.DeviceIdType.MESH
        )
    )
    for copy in coming:
        copy.start()
    for copy in coming:
        copy.wait()
    for r in range(2 * rows):
        potb[r] = jnp.broadcast_to(potf[pl.ds(r, 1), :], (GROUP, nz))

    cx, cy = circulant_row(nx), circulant_row(ny)
    centre = -0.5 * 3.0 * stencil_weights[0] + cx[0] + cy[0] - spectrum_center

    def shifted_sum(source, x):
        mid = source[pl.ds(x * ny, ny)]
        acc = zterm[pl.ds(x * ny, ny)] + (centre + potb[pl.ds(x * ny, ny)]) * mid
        for s in range(1, ny // 2 + 1):
            if cy[s]:
                beside = jnp.concatenate([mid[s:], mid[:s]], 0)
                if 2 * s != ny:
                    beside = beside + jnp.concatenate([mid[ny - s:], mid[: ny - s]], 0)
                acc = acc + np.float32(cy[s]) * beside
        for s in range(1, nx // 2 + 1):
            if cx[s]:
                beside = source[pl.ds((x + s) % nx * ny, ny)]
                if 2 * s != nx:
                    beside = beside + source[pl.ds((x - s) % nx * ny, ny)]
                acc = acc + np.float32(cx[s]) * beside
        return acc

    def z_pass(source):
        high, low = split(source[...].reshape(nx * ny * GROUP, nz))
        both = jnp.dot(jnp.concatenate([high, low], 1), zmat[...], preferred_element_type=jnp.float32)
        zterm[...] = (both[:, :nz] + both[:, nz:]).reshape(nx * ny, GROUP, nz)

    def spot(x, y, g):
        slab, r = x // (nx // 2), x % (nx // 2) * ny + y
        return pl.ds(slab * half + g * (GROUP * rows) + r, GROUP, stride=rows)

    def one_group(g, carry):
        mine = pl.ds(dom * (orbs // 2) + g * GROUP, GROUP)
        for x in range(nx):
            for y in range(ny):
                tcur[x * ny + y] = curf[spot(x, y, g), :]
        z_pass(tcur)
        c1, d1 = coef[0, mine], coef[1, mine]
        for x in range(nx):
            acc = shifted_sum(tcur, x)
            for y in range(ny):
                tmid[x * ny + y] = c1 * acc[y] - d1 * prevf[spot(x, y, g), :]
        z_pass(tmid)
        c2, d2 = coef[2, mine], coef[3, mine]
        for x in range(nx):
            acc = shifted_sum(tmid, x)
            for y in range(ny):
                full[spot(x, y, g), :] = c2 * acc[y] - d2 * tcur[x * ny + y]
        return carry

    lax.fori_loop(0, orbs // 2 // GROUP, one_group, 0)

    landing = own.at[pl.ds(dom * half, half)]
    keep = pltpu.make_async_copy(full.at[pl.ds(dom * half, half)], landing, back_local)
    back = pltpu.make_async_remote_copy(
        full.at[pl.ds(mate * half, half)], landing, back_send, back_recv,
        device_id={"dom": mate}, device_id_type=pl.DeviceIdType.MESH,
    )
    keep.start()
    back.start()
    keep.wait()
    back.wait()
    write = pltpu.make_async_copy(own, out, out_sem)
    write.start()

    def scatter(k):
        to = lax.rem(state + k, states)
        return pltpu.make_async_remote_copy(
            own.at[pl.ds(to * piece, piece)], slots.at[state], rs_send.at[to], rs_recv.at[state],
            device_id={"state": to}, device_id_type=pl.DeviceIdType.MESH,
        )

    def scatter_in(k):
        source = lax.rem(state + k, states)
        return pltpu.make_async_remote_copy(
            own.at[pl.ds(source * piece, piece)], slots.at[source], rs_send.at[source], rs_recv.at[source],
            device_id={"state": source}, device_id_type=pl.DeviceIdType.MESH,
        )

    def gather(k):
        to = lax.rem(state + k, states)
        mine = panel.at[pl.ds(state * piece, piece)]
        return pltpu.make_async_remote_copy(
            mine, mine, ag_send.at[to], ag_recv.at[state],
            device_id={"state": to}, device_id_type=pl.DeviceIdType.MESH,
        )

    def gather_in(k):
        source = lax.rem(state + k, states)
        theirs = panel.at[pl.ds(source * piece, piece)]
        return pltpu.make_async_remote_copy(
            theirs, theirs, ag_send.at[source], ag_recv.at[source],
            device_id={"state": source}, device_id_type=pl.DeviceIdType.MESH,
        )

    def each(action):
        def step(k, carry):
            action(k)
            return carry

        lax.fori_loop(1, states, step, 0)

    each(lambda k: scatter(k).start())
    keep = pltpu.make_async_copy(own.at[pl.ds(state * piece, piece)], slots.at[state], piece_sem)
    keep.start()

    for r in range(rows):
        high, low = split(own[pl.ds(r, orbs, stride=rows), :])
        parted[r] = jnp.concatenate([high, high, low], 1)

    keep.wait()
    each(lambda k: scatter_in(k).wait_recv())
    panel[pl.ds(state * piece, piece)] = slots[root_ref[0]]
    each(lambda k: gather(k).start())
    each(lambda k: gather_in(k).wait_recv())

    total = jnp.zeros((orbs, orbs), jnp.float32)
    for r in range(rows):
        high, low = split(panel[pl.ds(r, orbs, stride=rows), :])
        total = total + lax.dot_general(
            jnp.concatenate([high, low, high], 1), parted[r], (((1,), (1,)), ((), ())),
            preferred_element_type=jnp.float32,
        )
    partial[:, :orbs] = total * np.float32(1.0 / (nx * ny * nz))
    share = orbs // 2
    swap = pltpu.make_async_remote_copy(
        partial.at[pl.ds(mate * share, share)], other, sum_send, sum_recv,
        device_id={"dom": mate}, device_id_type=pl.DeviceIdType.MESH,
    )
    swap.start()
    swap.wait()
    margin[...] = partial[pl.ds(dom * share, share), :orbs] + other[:, :orbs]

    each(lambda k: scatter(k).wait_send())
    each(lambda k: gather(k).wait_send())
    write.wait()


def on_device(mesh, previous, current, potential, degree, panel_index):
    orbs, planes, ny, nz = previous.shape
    states = mesh.shape["state"]
    nx = planes * mesh.shape["dom"]
    rows = planes * ny
    sigma_now, sigma_next, sigma_after = sigma_table(degree)
    table = jnp.stack(
        [
            2.0 * sigma_next / spectrum_half,
            sigma_now * sigma_next,
            2.0 * sigma_after / spectrum_half,
            sigma_next * sigma_after,
        ]
    )
    coef = jnp.broadcast_to(table[:, :, None], (4, orbs, nz))
    zmat = jnp.asarray(z_matrix(nz))
    vmem, anyspace = pl.BlockSpec(memory_space=pltpu.VMEM), pl.BlockSpec(memory_space=pl.ANY)
    f32, bf16 = jnp.float32, jnp.bfloat16
    piece = orbs // states * rows
    dma = pltpu.SemaphoreType.DMA
    filtered, margin = pl.pallas_call(
        functools.partial(kernel, (orbs, nx, ny, nz, states)),
        out_shape=(
            jax.ShapeDtypeStruct((orbs * rows, nz), f32),
            jax.ShapeDtypeStruct((orbs // 2, orbs), f32),
        ),
        in_specs=[pl.BlockSpec(memory_space=pltpu.SMEM), anyspace, anyspace, anyspace, vmem, vmem],
        out_specs=(anyspace, vmem),
        scratch_shapes=[
            pltpu.VMEM((orbs * rows, nz), f32),
            pltpu.VMEM((orbs * rows, nz), f32),
            pltpu.VMEM((nx * ny, nz), f32),
            pltpu.VMEM((nx * ny, GROUP, nz), f32),
            pltpu.VMEM((nx * ny, GROUP, nz), f32),
            pltpu.VMEM((nx * ny, GROUP, nz), f32),
            pltpu.VMEM((nx * ny, GROUP, nz), f32),
            pltpu.VMEM((orbs * rows, nz), f32),
            pltpu.VMEM((orbs * rows, nz), f32),
            pltpu.VMEM((states, piece, nz), f32),
            pltpu.VMEM((orbs * rows, nz), f32),
            pltpu.VMEM((rows, orbs, 3 * nz), bf16),
            pltpu.VMEM((orbs, 128), f32),
            pltpu.VMEM((orbs // 2, 128), f32),
            dma((3,)), dma((3,)), dma((3,)), dma, dma, dma,
            dma((states,)), dma((states,)), dma((states,)), dma((states,)),
            dma, dma, dma, dma,
        ],
        compiler_params=pltpu.CompilerParams(
            collective_id=0, has_side_effects=True, vmem_limit_bytes=40 * 1024 * 1024
        ),
    )(
        panel_index,
        current.reshape(orbs * rows, nz),
        previous.reshape(orbs * rows, nz),
        potential.reshape(rows, nz),
        coef,
        zmat,
    )
    return filtered.reshape(previous.shape), margin


def solution(mesh):
    return jax.shard_map(
        functools.partial(on_device, mesh),
        mesh=mesh,
        in_specs=(
            P(("kpt", "state"), "dom", None, None),
            P(("kpt", "state"), "dom", None, None),
            P("dom", None, None),
            P(("kpt", "state")),
            P("kpt"),
        ),
        out_specs=(P(("kpt", "state"), "dom", None, None), P(("kpt", "dom"), "state")),
        check_vma=False,
    )
```

profile of v0, /device:TPU:31, one launch (start us, length us, event | category | flops | bytes accessed | tf_op | source)
XLA Modules:
  0.0 70.5 jit_solution(7167886518704641601)
XLA Ops:
  0.6 0.0 copy-start.2
  1.3 0.7 %multiply_bitcast_fusion.3 = (f32[1,64]{1,0:T(1,128)S(1)}, f32[64]{0:T(128)S(1)}, f32[64]{0:T(128)S(1)}) fusion(s32[64]{0:T(128)} %param.9), kind=kLoop, calls=%fused_computation.20 | loop fusion | flops 3904 | bytes 1024 | tf_op jit(solution)/shard_map/stack | solution.py:252
  2.1 0.0 copy-start.3
  2.1 0.1 broadcast_in_dim.10.coef
  2.2 0.0 copy-done.2
  2.2 0.6 copy-done.3
  2.8 0.0 copy-start
  2.8 1.2 %copy-done = f32[64,8,4,128]{3,2,1,0:T(4,128)S(1)} copy-done((f32[64,8,4,128]{3,2,1,0:T(4,128)S(1)}, f32[64,8,4,128]{3,2,1,0:T(4,128)}, u32[]{:S(2)}) %copy-start) | copy-done | bytes 1048600
  4.1 0.0 copy-start.1
  4.1 1.2 %copy-done.1 = f32[64,8,4,128]{3,2,1,0:T(4,128)S(1)} copy-done((f32[64,8,4,128]{3,2,1,0:T(4,128)S(1)}, f32[64,8,4,128]{3,2,1,0:T(4,128)}, u32[]{:S(2)}) %copy-start.1) | copy-done | bytes 1048600
  5.3 63.6 %shard_map.77 = (f32[2048,128]{1,0:T(8,128)S(1)}, f32[32,64]{1,0:T(8,128)S(1)}) custom-call(s32[1]{0:T(128)S(6)} %copy.10.root_ref, f32[2048,128]{1,0:T(8,128)S(1)} %bitcast.13, f32[2048,128]{1,0:T(8,128)S(1)} %bitcast.14, f32[32,128]{1,0:T(8,128)S(1)} %bitcast.15, f32[4,64,128]{2,1,0:T(8,128)S(1)} %broadcast_in_dim.10.coef, bf16[256,256]{1,0:T(8,128)(2,1)S(1)} %copy-done.2), custom_call_target="tpu_custom_call" | custom-call | tf_op jit(solution)/shard_map/pallas_call | solution.py:266
  68.9 1.0 %copy.11 = f32[64,8,4,128]{3,2,1,0:T(4,128)} copy(f32[64,8,4,128]{3,2,1,0:T(4,128)S(1)} %bitcast.12) | data formatting | bytes 2097152
  69.9 0.6 copy.12
  (3 shorter events, 0.0 us)
Async XLA Ops:
  0.6 1.6 %copy-start.2 = (bf16[256,256]{1,0:T(8,128)(2,1)S(1)}, bf16[256,256]{1,0:T(8,128)(2,1)}, u32[]{:S(2)}) copy-start(bf16[256,256]{1,0:T(8,128)(2,1)} %constant.47.clone.zmat) | copy-start | bytes 393220
  2.1 0.7 %copy-start.3 = (f32[8,4,128]{2,1,0:T(4,128)S(1)}, f32[8,4,128]{2,1,0:T(4,128)}, u32[]{:S(2)}) copy-start(f32[8,4,128]{2,1,0:T(4,128)} %param.8) | copy-start | bytes 49156
  2.8 1.2 %copy-start = (f32[64,8,4,128]{3,2,1,0:T(4,128)S(1)}, f32[64,8,4,128]{3,2,1,0:T(4,128)}, u32[]{:S(2)}) copy-start(f32[64,8,4,128]{3,2,1,0:T(4,128)} %param.7) | copy-start | bytes 3145732
  4.1 1.2 %copy-start.1 = (f32[64,8,4,128]{3,2,1,0:T(4,128)S(1)}, f32[64,8,4,128]{3,2,1,0:T(4,128)}, u32[]{:S(2)}) copy-start(f32[64,8,4,128]{3,2,1,0:T(4,128)} %param.6) | copy-start | bytes 3145732
where the time goes:
time: 70.7 us; the launch traced here: 70.5 us
  Pallas kernels  63.6 us (90%)
  local copies, waits for them, and re-layouts  4.73 us (7%)
  between operations  1.38 us (2%)
  other arithmetic  0.77 us (1%)
    pallas_call x1, Pallas kernels, on_device(): pl.pallas_call(functools.partial(kernel, (orbs, nx, ny, nz, states)), out...  63.6 us
    unnamed x10, local copies, waits for them, and re-layouts  4.64 us

commit v1 on v0

v1 whole, which is shorter than its diff:
```python
import functools

import jax
import jax.numpy as jnp
import numpy as np
from jax import lax
from jax.experimental import pallas as pl
from jax.experimental.pallas import tpu as pltpu
from jax.sharding import PartitionSpec as P

stencil_weights = (
    -5369.0 / 1800.0,
    12.0 / 7.0,
    -15.0 / 56.0,
    10.0 / 189.0,
    -1.0 / 112.0,
    2.0 / 1925.0,
    -1.0 / 16632.0,
)
spectrum_center = 8.0
spectrum_half = 8.0
first_ratio = 8.0 / (-0.5 - 8.0)
inverse_two = 2.0 / first_ratio
GROUP = 8
CUTS = 2


def sigma_table(degree):
    sigma_now = jnp.full(degree.shape, first_ratio, jnp.float32)
    for repeat in range(1, 16):
        sigma_now = jnp.where(repeat < degree, 1.0 / (inverse_two - sigma_now), sigma_now)
    sigma_next = 1.0 / (inverse_two - sigma_now)
    sigma_after = 1.0 / (inverse_two - sigma_next)
    return (sigma_now, sigma_next, sigma_after)


def circulant_row(length):
    row = np.zeros(length)
    for m in range(1, len(stencil_weights)):
        row[m % length] += -0.5 * stencil_weights[m]
        row[-m % length] += -0.5 * stencil_weights[m]
    return row


def z_matrix(length):
    row = circulant_row(length)
    full = np.stack([np.roll(row, i) for i in range(length)]).astype(np.float32)
    high = full.astype(jnp.bfloat16)
    low = (full - high.astype(np.float32)).astype(jnp.bfloat16)
    zero = np.zeros_like(high)
    return np.block([[high, low], [high, zero]])


def split(value):
    high = value.astype(jnp.bfloat16)
    low = (value - high.astype(jnp.float32)).astype(jnp.bfloat16)
    return high, low


def kernel(
    sizes,
    root_ref, cur, prev, pot, coef, zmat, out, margin,
    curf, prevf, potf, potb, tcur, tmid, zterm, own, before, chosen, up_in, up_out, down_in, down_out,
    panel, parted, partial, other,
    in_local, in_send, in_recv, back_send, back_recv, pre_send, pre_recv, up_send, up_recv,
    down_send, down_recv, post_send, post_recv, out_sem, sum_send, sum_recv,
):
    orbs, nx, ny, nz, states = sizes
    rows = nx // 2 * ny
    half = orbs // 2 * rows
    groups = orbs // 2 // GROUP
    span = GROUP * rows
    chunks = groups * CUTS
    block = span // CUTS
    dom, state = lax.axis_index("dom"), lax.axis_index("state")
    mate = 1 - dom
    line, b = state // 2, lax.rem(state, 2)
    count = states // 2
    peer = line * 2 + 1 - b

    barrier = pltpu.get_barrier_semaphore()

    def greet(where):
        pl.semaphore_signal(barrier, 1, device_id=where, device_id_type=pl.DeviceIdType.MESH)

    greet({"dom": mate})
    greet({"state": peer})

    @pl.when(line > 0)
    def _():
        greet({"state": state - 2})

    @pl.when(line < count - 1)
    def _():
        greet({"state": state + 2})

    @pl.when(line == 0)
    def _():
        up_in[...] = jnp.zeros_like(up_in)

    @pl.when(line == count - 1)
    def _():
        down_in[...] = jnp.zeros_like(down_in)

    pl.semaphore_wait(barrier, 4 - (line == 0).astype(jnp.int32) - (line == count - 1).astype(jnp.int32))

    def remote(source, target, send, recv, where):
        return pltpu.make_async_remote_copy(
            source, target, send, recv, device_id=where, device_id_type=pl.DeviceIdType.MESH
        )

    here = potf.at[pl.ds(dom * rows, rows)]
    pot_copies = (
        pltpu.make_async_copy(pot, here, in_local.at[2 * groups]),
        remote(pot, here, in_send.at[2 * groups], in_recv.at[2 * groups], {"dom": mate}),
    )

    def coming(g):
        copies = []
        for i, (source, target) in enumerate(((cur, curf), (prev, prevf))):
            here = target.at[pl.ds(dom * half + g * span, span)]
            n = 2 * g + i
            copies.append(
                remote(
                    source.at[pl.ds(mate * half + g * span, span)], here, in_send.at[n], in_recv.at[n], {"dom": mate}
                )
            )
            copies.append(
                pltpu.make_async_copy(source.at[pl.ds(dom * half + g * span, span)], here, in_local.at[n])
            )
        return copies

    for copy in pot_copies:
        copy.start()
    for g in range(groups):
        for copy in coming(g):
            copy.start()
    for copy in pot_copies:
        copy.wait()
    for r in range(2 * rows):
        potb[r] = jnp.broadcast_to(potf[pl.ds(r, 1), :], (GROUP, nz))

    cx, cy = circulant_row(nx), circulant_row(ny)
    centre = -0.5 * 3.0 * stencil_weights[0] + cx[0] + cy[0] - spectrum_center

    def shifted_sum(source, x):
        mid = source[pl.ds(x * ny, ny)]
        acc = zterm[pl.ds(x * ny, ny)] + (centre + potb[pl.ds(x * ny, ny)]) * mid
        for s in range(1, ny // 2 + 1):
            if cy[s]:
                beside = jnp.concatenate([mid[s:], mid[:s]], 0)
                if 2 * s != ny:
                    beside = beside + jnp.concatenate([mid[ny - s:], mid[: ny - s]], 0)
                acc = acc + np.float32(cy[s]) * beside
        for s in range(1, nx // 2 + 1):
            if cx[s]:
                beside = source[pl.ds((x + s) % nx * ny, ny)]
                if 2 * s != nx:
                    beside = beside + source[pl.ds((x - s) % nx * ny, ny)]
                acc = acc + np.float32(cx[s]) * beside
        return acc

    def z_pass(source):
        high, low = split(source[...].reshape(nx * ny * GROUP, nz))
        both = jnp.dot(jnp.concatenate([high, low], 1), zmat[...], preferred_element_type=jnp.float32)
        zterm[...] = (both[:, :nz] + both[:, nz:]).reshape(nx * ny, GROUP, nz)

    def spot(x, y, g):
        slab, r = x // (nx // 2), x % (nx // 2) * ny + y
        return pl.ds(slab * half + g * span + r, GROUP, stride=rows)

    def result_spot(x, y, g):
        slab, r = x // (nx // 2), x % (nx // 2) * ny + y
        start = (2 - dom) * half if slab else dom * 2 * half
        return pl.ds(start + g * span + r, GROUP, stride=rows)

    def back(g):
        return remote(
            own.at[pl.ds(2 * half + g * span, span)], own.at[pl.ds(dom * half + g * span, span)],
            back_send.at[g], back_recv.at[g], {"dom": mate},
        )

    def pre(c):
        return remote(
            own.at[pl.ds((1 - b) * half + c * block, block)], before.at[c],
            pre_send.at[c], pre_recv.at[c], {"state": peer},
        )

    def hand_over(g):
        back(g).wait_recv()
        for i in range(CUTS):
            pre(g * CUTS + i).start()

    def one_group(g, carry):
        for copy in coming(g):
            copy.wait()
        mine = pl.ds(dom * (orbs // 2) + g * GROUP, GROUP)
        for x in range(nx):
            for y in range(ny):
                tcur[x * ny + y] = curf[spot(x, y, g), :]
        z_pass(tcur)
        c1, d1 = coef[0, mine], coef[1, mine]
        for x in range(nx):
            acc = shifted_sum(tcur, x)
            for y in range(ny):
                tmid[x * ny + y] = c1 * acc[y] - d1 * prevf[spot(x, y, g), :]
        z_pass(tmid)
        c2, d2 = coef[2, mine], coef[3, mine]
        for x in range(nx):
            acc = shifted_sum(tmid, x)
            for y in range(ny):
                own[result_spot(x, y, g), :] = c2 * acc[y] - d2 * tcur[x * ny + y]
        back(g).start()

        @pl.when(g > 0)
        def _():
            hand_over(g - 1)

        return carry

    lax.fori_loop(0, groups, one_group, 0)
    hand_over(groups - 1)
    write = pltpu.make_async_copy(own.at[pl.ds(0, 2 * half)], out, out_sem)
    write.start()

    root = root_ref[0]
    root_line, root_b = root // 2, lax.rem(root, 2)

    def up(c):
        return remote(up_out.at[c], up_in.at[c], up_send.at[c], up_recv.at[c], {"state": state + 2})

    def down(c):
        return remote(down_out.at[c], down_in.at[c], down_send.at[c], down_recv.at[c], {"state": state - 2})

    def post(c):
        place = panel.at[pl.ds(b * half + c * block, block)]
        return remote(place, place, post_send.at[c], post_recv.at[c], {"state": peer})

    near = jnp.minimum(line, count - 1 - line)
    far = jnp.maximum(line, count - 1 - line)

    def at_step(c, action):
        @pl.when((c >= 0) & (c < chunks))
        def _():
            action(c)

    def choose(c):
        pre(c).wait_recv()
        chosen[c] = jnp.where(root_b == b, own[pl.ds(b * half + c * block, block), :], before[c])

    def go_up(c):
        @pl.when(line > 0)
        def _():
            up(c).wait_recv()

        @pl.when(line < count - 1)
        def _():
            up_out[c] = jnp.where(root_line == line, chosen[c], up_in[c])
            up(c).start()

    def go_down(c):
        @pl.when(line < count - 1)
        def _():
            down(c).wait_recv()

        @pl.when(line > 0)
        def _():
            down_out[c] = jnp.where(root_line == line, chosen[c], down_in[c])
            down(c).start()

    def finish(c):
        arrived = jnp.where(root_line < line, up_in[c], down_in[c])
        panel[pl.ds(b * half + c * block, block), :] = jnp.where(root_line == line, chosen[c], arrived)
        post(c).start()

    def wave(t, carry):
        at_step(t - near, choose)
        at_step(t - line, go_up)
        at_step(t - (count - 1 - line), go_down)
        at_step(t - far, finish)
        return carry

    lax.fori_loop(0, chunks + count - 1, wave, 0)

    for r in range(rows):
        high, low = split(own[pl.ds(r, orbs, stride=rows), :])
        parted[r] = jnp.concatenate([high, high, low], 1)

    def every(size, action):
        def step(c, carry):
            action(c)
            return carry

        lax.fori_loop(0, size, step, 0)

    def post_in(c):
        place = panel.at[pl.ds((1 - b) * half + c * block, block)]
        return remote(place, place, post_send.at[c], post_recv.at[c], {"state": peer})

    every(chunks, lambda c: post_in(c).wait_recv())

    total = jnp.zeros((orbs, orbs), jnp.float32)
    for r in range(rows):
        high, low = split(panel[pl.ds(r, orbs, stride=rows), :])
        total = total + lax.dot_general(
            jnp.concatenate([high, low, high], 1), parted[r], (((1,), (1,)), ((), ())),
            preferred_element_type=jnp.float32,
        )
    partial[:, :orbs] = total * np.float32(1.0 / (nx * ny * nz))
    share = orbs // 2
    swap = remote(partial.at[pl.ds(mate * share, share)], other, sum_send, sum_recv, {"dom": mate})
    swap.start()
    swap.wait()
    margin[...] = partial[pl.ds(dom * share, share), :orbs] + other[:, :orbs]

    every(groups, lambda g: back(g).wait_send())

    def sent(c):
        pre(c).wait_send()
        post(c).wait_send()

        @pl.when(line < count - 1)
        def _():
            up(c).wait_send()

        @pl.when(line > 0)
        def _():
            down(c).wait_send()

    every(chunks, sent)
    write.wait()


def on_device(mesh, previous, current, potential, degree, panel_index):
    orbs, planes, ny, nz = previous.shape
    states = mesh.shape["state"]
    nx = planes * mesh.shape["dom"]
    rows = planes * ny
    sigma_now, sigma_next, sigma_after = sigma_table(degree)
    table = jnp.stack(
        [
            2.0 * sigma_next / spectrum_half,
            sigma_now * sigma_next,
            2.0 * sigma_after / spectrum_half,
            sigma_next * sigma_after,
        ]
    )
    coef = jnp.broadcast_to(table[:, :, None], (4, orbs, nz))
    zmat = jnp.asarray(z_matrix(nz))
    vmem, anyspace = pl.BlockSpec(memory_space=pltpu.VMEM), pl.BlockSpec(memory_space=pl.ANY)
    f32, bf16 = jnp.float32, jnp.bfloat16
    groups = orbs // 2 // GROUP
    chunks = groups * CUTS
    block = GROUP * rows // CUTS
    dma = pltpu.SemaphoreType.DMA
    filtered, margin = pl.pallas_call(
        functools.partial(kernel, (orbs, nx, ny, nz, states)),
        out_shape=(
            jax.ShapeDtypeStruct((orbs * rows, nz), f32),
            jax.ShapeDtypeStruct((orbs // 2, orbs), f32),
        ),
        in_specs=[pl.BlockSpec(memory_space=pltpu.SMEM), anyspace, anyspace, anyspace, vmem, vmem],
        out_specs=(anyspace, vmem),
        scratch_shapes=[
            pltpu.VMEM((orbs * rows, nz), f32),
            pltpu.VMEM((orbs * rows, nz), f32),
            pltpu.VMEM((nx * ny, nz), f32),
            pltpu.VMEM((nx * ny, GROUP, nz), f32),
            pltpu.VMEM((nx * ny, GROUP, nz), f32),
            pltpu.VMEM((nx * ny, GROUP, nz), f32),
            pltpu.VMEM((nx * ny, GROUP, nz), f32),
            pltpu.VMEM((orbs * rows * 3 // 2, nz), f32),
            *[pltpu.VMEM((chunks, block, nz), f32)] * 6,
            pltpu.VMEM((orbs * rows, nz), f32),
            pltpu.VMEM((rows, orbs, 3 * nz), bf16),
            pltpu.VMEM((orbs, 128), f32),
            pltpu.VMEM((orbs // 2, 128), f32),
            *[dma((2 * groups + 1,))] * 3,
            *[dma((groups,))] * 2,
            *[dma((chunks,))] * 8,
            dma, dma, dma,
        ],
        compiler_params=pltpu.CompilerParams(
            collective_id=0, has_side_effects=True, vmem_limit_bytes=60 * 1024 * 1024
        ),
    )(
        panel_index,
        current.reshape(orbs * rows, nz),
        previous.reshape(orbs * rows, nz),
        potential.reshape(rows, nz),
        coef,
        zmat,
    )
    return filtered.reshape(previous.shape), margin


def solution(mesh):
    return jax.shard_map(
        functools.partial(on_device, mesh),
        mesh=mesh,
        in_specs=(
            P(("kpt", "state"), "dom", None, None),
            P(("kpt", "state"), "dom", None, None),
            P("dom", None, None),
            P(("kpt", "state")),
            P("kpt"),
        ),
        out_specs=(P(("kpt", "state"), "dom", None, None), P(("kpt", "dom"), "state")),
        check_vma=False,
    )
```

time: 70.7 us -> 56.5 us (0.80)
  the two profiles are of different devices: /device:TPU:31 before, /device:TPU:0 now
where the time goes in v1:
time: 56.5 us; the launch traced here: 56.2 us
  Pallas kernels  50.5 us (89%)
  local copies, waits for them, and re-layouts  4.29 us (8%)
  between operations  1.33 us (2%)
    pallas_call x1, Pallas kernels, on_device(): pl.pallas_call(functools.partial(kernel, (orbs, nx, ny, nz, states)), out...  50.5 us
    unnamed x6, local copies, waits for them, and re-layouts  3.53 us

profile of v1, /device:TPU:0, one launch (start us, length us, event | category | flops | bytes accessed | tf_op | source)
XLA Modules:
  0.0 56.2 jit_solution(13257336963021426837)
XLA Ops:
  1.3 0.0 copy-start.1
  1.3 0.6 %copy-done.1 = s32[64]{0:T(128)S(1)} copy-done((s32[64]{0:T(128)S(1)}, s32[64]{0:T(128)}, u32[]{:S(2)}) %copy-start.1) | copy-done | bytes 280
  1.9 0.1 multiply_bitcast_fusion.3
  2.1 0.8 %broadcast_in_dim.10.coef = f32[4,64,128]{2,1,0:T(8,128)} broadcast(f32[4,64]{1,0:T(4,128)S(1)} %pad_maximum_fusion), dimensions={0,1} | broadcast | bytes 132096 | tf_op jit(solution)/shard_map/broadcast_in_dim | solution.py:348
  2.8 50.5 %shard_map.77 = (f32[2048,128]{1,0:T(8,128)}, f32[32,64]{1,0:T(8,128)}) custom-call(s32[1]{0:T(128)S(6)} %copy.10.root_ref, f32[2048,128]{1,0:T(8,128)} %bitcast.13, f32[2048,128]{1,0:T(8,128)} %bitcast.14, f32[32,128]{1,0:T(8,128)} %bitcast.15, f32[4,64,128]{2,1,0:T(8,128)} %broadcast_in_dim.10.coef, bf16[256,256]{1,0:T(8,128)(2,1)} %constant.47.clone.zmat), custom_call_target="tpu_custom_call" | custom-call | tf_op jit(solution)/shard_map/pallas_call | solution.py:356
  53.3 0.0 copy-start
  53.3 2.3 %copy.11 = f32[64,8,4,128]{3,2,1,0:T(4,128)} copy(f32[64,8,4,128]{3,2,1,0:T(4,128)} %bitcast.12) | data formatting | bytes 2097152
  55.6 0.0 copy-done
  55.6 0.6 %copy.12 = f32[32,64]{1,0:T(8,128)} copy(f32[32,64]{1,0:T(8,128)S(1)} %copy-done) | data formatting | bytes 16384
  (3 shorter events, 0.0 us)
Async XLA Ops:
  1.3 0.7 %copy-start.1 = (s32[64]{0:T(128)S(1)}, s32[64]{0:T(128)}, u32[]{:S(2)}) copy-start(s32[64]{0:T(128)} %param.9) | copy-start | bytes 772
  53.3 2.3 %copy-start = (f32[32,64]{1,0:T(8,128)S(1)}, f32[32,64]{1,0:T(8,128)}, u32[]{:S(2)}) copy-start(f32[32,64]{1,0:T(8,128)} %get-tuple-element.15) | copy-start | bytes 24580

commit v2 on v1

--- a/solution.py
+++ b/solution.py
@@ -23,6 +23,7 @@
 inverse_two = 2.0 / first_ratio
 GROUP = 8
 CUTS = 2
+SKEW = 3
 
 
 def sigma_table(degree):
@@ -42,24 +43,41 @@
     return row
 
 
-def z_matrix(length):
-    row = circulant_row(length)
-    full = np.stack([np.roll(row, i) for i in range(length)]).astype(np.float32)
-    high = full.astype(jnp.bfloat16)
-    low = (full - high.astype(np.float32)).astype(jnp.bfloat16)
-    zero = np.zeros_like(high)
-    return np.block([[high, low], [high, zero]])
-
-
 def split(value):
     high = value.astype(jnp.bfloat16)
     low = (value - high.astype(jnp.float32)).astype(jnp.bfloat16)
     return high, low
 
 
+def fill_z_matrix(zmat, length):
+    row = circulant_row(length)
+    shape = (length, length)
+    apart = lax.broadcasted_iota(jnp.int32, shape, 0) - lax.broadcasted_iota(jnp.int32, shape, 1)
+    apart = jnp.where(apart < 0, apart + length, apart)
+    full = jnp.zeros(shape, jnp.float32)
+    for s in range(length):
+        if row[s]:
+            full = jnp.where(apart == s, np.float32(row[s]), full)
+    high, low = split(full)
+    top = jnp.concatenate([high, low], 1)
+    zmat[...] = jnp.concatenate([top, jnp.concatenate([high, jnp.zeros_like(low)], 1)], 0)
+
+
+def fill_coefficients(coef, degree, width):
+    now, following, after = sigma_table(degree)
+    orbs = degree.shape[1]
+    shape = (orbs, orbs)
+    diagonal = lax.broadcasted_iota(jnp.int32, shape, 0) == lax.broadcasted_iota(jnp.int32, shape, 1)
+    for i, line in enumerate(
+        (2.0 * following / spectrum_half, now * following, 2.0 * after / spectrum_half, following * after)
+    ):
+        column = jnp.sum(jnp.where(diagonal, jnp.broadcast_to(line, shape), 0.0), axis=1, keepdims=True)
+        coef[i] = jnp.broadcast_to(column, (orbs, width))
+
+
 def kernel(
     sizes,
-    root_ref, cur, prev, pot, coef, zmat, out, margin,
+    root_ref, degree, cur, prev, pot, out, margin, coef, zmat,
     curf, prevf, potf, potb, tcur, tmid, zterm, own, before, chosen, up_in, up_out, down_in, down_out,
     panel, parted, partial, other,
     in_local, in_send, in_recv, back_send, back_recv, pre_send, pre_recv, up_send, up_recv,
@@ -102,6 +120,7 @@
     def _():
         down_in[...] = jnp.zeros_like(down_in)
 
+    fill_z_matrix(zmat, nz)
     pl.semaphore_wait(barrier, 4 - (line == 0).astype(jnp.int32) - (line == count - 1).astype(jnp.int32))
 
     def remote(source, target, send, recv, where):
@@ -135,6 +154,7 @@
     for g in range(groups):
         for copy in coming(g):
             copy.start()
+    fill_coefficients(coef, degree[...], nz)
     for copy in pot_copies:
         copy.wait()
     for r in range(2 * rows):
@@ -187,7 +207,6 @@
         )
 
     def hand_over(g):
-        back(g).wait_recv()
         for i in range(CUTS):
             pre(g * CUTS + i).start()
 
@@ -212,14 +231,29 @@
                 own[result_spot(x, y, g), :] = c2 * acc[y] - d2 * tcur[x * ny + y]
         back(g).start()
 
-        @pl.when(g > 0)
-        def _():
+        @pl.when(dom != b)
+        def _():
+            hand_over(g)
+
+        @pl.when((dom == b) & (g > 0))
+        def _():
+            back(g - 1).wait_recv()
             hand_over(g - 1)
 
         return carry
 
     lax.fori_loop(0, groups, one_group, 0)
-    hand_over(groups - 1)
+
+    @pl.when(dom == b)
+    def _():
+        back(groups - 1).wait_recv()
+        hand_over(groups - 1)
+
+    @pl.when(dom != b)
+    def _():
+        for g in range(groups):
+            back(g).wait_recv()
+
     write = pltpu.make_async_copy(own.at[pl.ds(0, 2 * half)], out, out_sem)
     write.start()
 
@@ -236,8 +270,8 @@
         place = panel.at[pl.ds(b * half + c * block, block)]
         return remote(place, place, post_send.at[c], post_recv.at[c], {"state": peer})
 
-    near = jnp.minimum(line, count - 1 - line)
-    far = jnp.maximum(line, count - 1 - line)
+    below, above = SKEW * line, SKEW * (count - 1 - line)
+    near, far = jnp.minimum(below, above), jnp.maximum(below, above)
 
     def at_step(c, action):
         @pl.when((c >= 0) & (c < chunks))
@@ -275,12 +309,12 @@
 
     def wave(t, carry):
         at_step(t - near, choose)
-        at_step(t - line, go_up)
-        at_step(t - (count - 1 - line), go_down)
+        at_step(t - below, go_up)
+        at_step(t - above, go_down)
         at_step(t - far, finish)
         return carry
 
-    lax.fori_loop(0, chunks + count - 1, wave, 0)
+    lax.fori_loop(0, chunks + SKEW * (count - 1), wave, 0)
 
     for r in range(rows):
         high, low = split(own[pl.ds(r, orbs, stride=rows), :])
@@ -336,18 +370,8 @@
     states = mesh.shape["state"]
     nx = planes * mesh.shape["dom"]
     rows = planes * ny
-    sigma_now, sigma_next, sigma_after = sigma_table(degree)
-    table = jnp.stack(
-        [
-            2.0 * sigma_next / spectrum_half,
-            sigma_now * sigma_next,
-            2.0 * sigma_after / spectrum_half,
-            sigma_next * sigma_after,
-        ]
-    )
-    coef = jnp.broadcast_to(table[:, :, None], (4, orbs, nz))
-    zmat = jnp.asarray(z_matrix(nz))
     vmem, anyspace = pl.BlockSpec(memory_space=pltpu.VMEM), pl.BlockSpec(memory_space=pl.ANY)
+    hbm = pl.BlockSpec(memory_space=pltpu.HBM)
     f32, bf16 = jnp.float32, jnp.bfloat16
     groups = orbs // 2 // GROUP
     chunks = groups * CUTS
@@ -359,9 +383,11 @@
             jax.ShapeDtypeStruct((orbs * rows, nz), f32),
             jax.ShapeDtypeStruct((orbs // 2, orbs), f32),
         ),
-        in_specs=[pl.BlockSpec(memory_space=pltpu.SMEM), anyspace, anyspace, anyspace, vmem, vmem],
+        in_specs=[pl.BlockSpec(memory_space=pltpu.SMEM), vmem, hbm, hbm, hbm],
         out_specs=(anyspace, vmem),
         scratch_shapes=[
+            pltpu.VMEM((4, orbs, nz), f32),
+            pltpu.VMEM((2 * nz, 2 * nz), bf16),
             pltpu.VMEM((orbs * rows, nz), f32),
             pltpu.VMEM((orbs * rows, nz), f32),
             pltpu.VMEM((nx * ny, nz), f32),
@@ -385,11 +411,10 @@
         ),
     )(
         panel_index,
+        degree.reshape(1, orbs),
         current.reshape(orbs * rows, nz),
         previous.reshape(orbs * rows, nz),
         potential.reshape(rows, nz),
-        coef,
-        zmat,
     )
     return filtered.reshape(previous.shape), margin
 

time: 56.5 us -> 43.2 us (0.76)
  Pallas kernels: 50.5 us -> 38.7 us
  local copies, waits for them, and re-layouts: 4.29 us -> 2.88 us
    pallas_call x1, Pallas kernels: 50.5 us -> 38.7 us  [on_device(): pl.pallas_call(functools.partial(kernel, (orbs, nx, ny, nz, states)), out...]
    broadcast_in_dim x1 -> x0, local copies, waits for them, and re-layouts: 0.76 us -> none  [on_device(): coef = jnp.broadcast_to(table[:, :, None], (4, orbs, nz))]
    unnamed x6 -> x4, local copies, waits for them, and re-layouts: 3.53 us -> 2.88 us
where the time goes in v2:
time: 43.2 us; the launch traced here: 42.9 us
  Pallas kernels  38.7 us (90%)
  local copies, waits for them, and re-layouts  2.88 us (7%)
  between operations  1.29 us (3%)
    pallas_call x1, Pallas kernels, on_device(): pl.pallas_call(functools.partial(kernel, (orbs, nx, ny, nz, states)), out...  38.7 us
    unnamed x4, local copies, waits for them, and re-layouts  2.88 us

profile of v2, /device:TPU:0, one launch (start us, length us, event | category | flops | bytes accessed | tf_op | source)
XLA Modules:
  0.0 42.9 jit_solution(9239212475568840384)
XLA Ops:
  1.3 38.7 %shard_map.68 = (f32[2048,128]{1,0:T(8,128)}, f32[32,64]{1,0:T(8,128)}) custom-call(s32[1]{0:T(128)S(6)} %copy.9.root_ref, s32[1,64]{1,0:T(1,128)} %bitcast.9, f32[2048,128]{1,0:T(8,128)} %bitcast.6, f32[2048,128]{1,0:T(8,128)} %bitcast.7, f32[32,128]{1,0:T(8,128)} %bitcast.8), custom_call_target="tpu_custom_call" | custom-call | tf_op jit(solution)/shard_map/pallas_call | solution.py:380
  40.0 0.0 copy-start
  40.0 2.3 %copy.10 = f32[64,8,4,128]{3,2,1,0:T(4,128)} copy(f32[64,8,4,128]{3,2,1,0:T(4,128)} %bitcast.5) | data formatting | bytes 2097152
  42.3 0.0 copy-done
  42.3 0.6 %copy.11 = f32[32,64]{1,0:T(8,128)} copy(f32[32,64]{1,0:T(8,128)S(1)} %copy-done) | data formatting | bytes 16384
Async XLA Ops:
  40.0 2.3 %copy-start = (f32[32,64]{1,0:T(8,128)S(1)}, f32[32,64]{1,0:T(8,128)}, u32[]{:S(2)}) copy-start(f32[32,64]{1,0:T(8,128)} %get-tuple-element.9) | copy-start | bytes 24580

commit v3 on v2

--- a/solution.py
+++ b/solution.py
@@ -22,8 +22,8 @@
 first_ratio = 8.0 / (-0.5 - 8.0)
 inverse_two = 2.0 / first_ratio
 GROUP = 8
-CUTS = 2
-SKEW = 3
+CUTS = 4
+SKEW = 5
 
 
 def sigma_table(degree):
@@ -331,16 +331,19 @@
         place = panel.at[pl.ds((1 - b) * half + c * block, block)]
         return remote(place, place, post_send.at[c], post_recv.at[c], {"state": peer})
 
+    def products(which):
+        total = jnp.zeros((orbs // 2, orbs), jnp.float32)
+        for r in range(rows):
+            high, low = split(panel[pl.ds(which * half + r, orbs // 2, stride=rows), :])
+            total = total + lax.dot_general(
+                jnp.concatenate([high, low, high], 1), parted[r], (((1,), (1,)), ((), ())),
+                preferred_element_type=jnp.float32,
+            )
+        partial[pl.ds(which * (orbs // 2), orbs // 2), :orbs] = total * np.float32(1.0 / (nx * ny * nz))
+
+    products(b)
     every(chunks, lambda c: post_in(c).wait_recv())
-
-    total = jnp.zeros((orbs, orbs), jnp.float32)
-    for r in range(rows):
-        high, low = split(panel[pl.ds(r, orbs, stride=rows), :])
-        total = total + lax.dot_general(
-            jnp.concatenate([high, low, high], 1), parted[r], (((1,), (1,)), ((), ())),
-            preferred_element_type=jnp.float32,
-        )
-    partial[:, :orbs] = total * np.float32(1.0 / (nx * ny * nz))
+    products(1 - b)
     share = orbs // 2
     swap = remote(partial.at[pl.ds(mate * share, share)], other, sum_send, sum_recv, {"dom": mate})
     swap.start()

time: 43.2 us -> 42 us (0.972)
  Pallas kernels: 38.7 us -> 37.5 us
    pallas_call x1, Pallas kernels: 38.7 us -> 37.5 us  [on_device(): pl.pallas_call(functools.partial(kernel, (orbs, nx, ny, nz, states)), out...]
where the time goes in v3:
time: 42 us; the launch traced here: 41.7 us
  Pallas kernels  37.5 us (89%)
  local copies, waits for them, and re-layouts  2.88 us (7%)
  between operations  1.29 us (3%)
    pallas_call x1, Pallas kernels, on_device(): pl.pallas_call(functools.partial(kernel, (orbs, nx, ny, nz, states)), out...  37.5 us
    unnamed x4, local copies, waits for them, and re-layouts  2.88 us

profile of v3, /device:TPU:0, one launch (start us, length us, event | category | flops | bytes accessed | tf_op | source)
XLA Modules:
  0.0 41.7 jit_solution(9934647992972575788)
XLA Ops:
  1.3 37.5 %shard_map.68 = (f32[2048,128]{1,0:T(8,128)}, f32[32,64]{1,0:T(8,128)}) custom-call(s32[1]{0:T(128)S(6)} %copy.9.root_ref, s32[1,64]{1,0:T(1,128)} %bitcast.9, f32[2048,128]{1,0:T(8,128)} %bitcast.6, f32[2048,128]{1,0:T(8,128)} %bitcast.7, f32[32,128]{1,0:T(8,128)} %bitcast.8), custom_call_target="tpu_custom_call" | custom-call | tf_op jit(solution)/shard_map/pallas_call | solution.py:383
  38.8 0.0 copy-start
  38.8 2.3 %copy.10 = f32[64,8,4,128]{3,2,1,0:T(4,128)} copy(f32[64,8,4,128]{3,2,1,0:T(4,128)} %bitcast.5) | data formatting | bytes 2097152
  41.1 0.0 copy-done
  41.1 0.6 %copy.11 = f32[32,64]{1,0:T(8,128)} copy(f32[32,64]{1,0:T(8,128)S(1)} %copy-done) | data formatting | bytes 16384
Async XLA Ops:
  38.8 2.3 %copy-start = (f32[32,64]{1,0:T(8,128)S(1)}, f32[32,64]{1,0:T(8,128)}, u32[]{:S(2)}) copy-start(f32[32,64]{1,0:T(8,128)} %get-tuple-element.9) | copy-start | bytes 24580
